TPU v7x, 512 devices: a whole 4x8x8 slice. The times are simulated.
512 devices in a mesh: ctx: 128 (over z, y, core), head: 4 (over x).
Axes of the slice: x: 4, y: 8, z: 8, core: 2. Of those that a mesh axis runs over, the one named last changes fastest.
Arguments:
- features: bfloat16 [32768, 1024], P('ctx', 'head'), may hold values from -30 to 30
- w_qkv: bfloat16 [1024, 3, 1024], P(None, None, 'head'), may hold values from -1 to 1
- block_links: int32 [256, 9], P('ctx'), may hold values from -1 to 255, as said below
- d_out: bfloat16 [32768, 1024], P('ctx', 'head'), may hold values from -6 to 6
Outputs:
- attended: bfloat16 [32768, 1024], P('ctx', 'head')
- grad_features: bfloat16 [32768, 1024], P('ctx', 'head')
Inputs may be any that keep to these rules, and one draw needn't show every extreme that they name: `block_links`: row q lists in order the key blocks q - 1 to q + 1; then p - 1 to p + 1, p being the block on the previous coil turn; then n - 1 to n + 1, n being the block on the next coil turn. q - p and n - q lie between 3 and 5, and a distance of 5 occurs in both directions in every draw. A coil neighbour may be absent; the entries of an absent neighbour and entries outside the sequence are -1. Live entries of a row are distinct.
All inputs are finite; a program needn't handle non-finite values.
Results may differ from a plain program's by a relative error of at most 0.025.
Values may be sent and summed in bfloat16 or wider, within the bound.
A program may use at most 64 MiB of HBM per device.

v0:
```python
import jax
import jax.numpy as jnp
from jax import lax
from jax.sharding import PartitionSpec as P

HD = 128
BLK = 128
OMAX = 3


def shifted(value, axis, steps):
    count = lax.axis_size(axis)
    first, last = (max(0, -steps), min(count, count - steps))
    return lax.ppermute(value, axis, [(source, source + steps) for source in range(first, last)])


def rounded_terms(values):
    return lax.optimization_barrier(values.astype(jnp.bfloat16)).astype(jnp.float32)


def body(features, w_qkv, block_links, d_out):
    tok_rows = d_out.shape[0]
    local_width = w_qkv.shape[2]
    model_width = w_qkv.shape[0]
    resident_tiles = tok_rows // BLK
    heads_here = local_width // HD
    score_scale = HD ** (-0.5)
    w_flat = w_qkv.reshape(model_width, 3 * local_width)
    projected = jnp.dot(
        lax.all_gather(features, "head", axis=1, tiled=True),
        w_flat,
        preferred_element_type=jnp.float32,
    )
    projected = projected.astype(jnp.bfloat16)
    query_blocks = projected[:, :local_width].reshape(resident_tiles, BLK, heads_here, HD)
    pair_blocks = projected[:, local_width:].reshape(resident_tiles, BLK, 2 * local_width)
    lower_shards = []
    upper_shards = []
    for offset in range(1, OMAX + 1):
        for direction in (1, -1):
            arrived = shifted(pair_blocks, "ctx", direction * offset)
            if direction > 0:
                lower_shards.append(arrived)
            else:
                upper_shards.append(arrived)
    window_pairs = jnp.concatenate(
        list(reversed(lower_shards)) + [pair_blocks] + upper_shards, axis=0
    )
    extent = window_pairs.shape[0]
    own_start = OMAX * resident_tiles
    anchor = lax.axis_index("ctx") * resident_tiles - own_start
    live_slot = block_links >= 0
    slot_index = jnp.where(live_slot, block_links - anchor, own_start)
    drop_index = jnp.where(live_slot, block_links - anchor, extent)
    slots = block_links.shape[1]
    selected = window_pairs[slot_index].reshape(resident_tiles, slots * BLK, 2, heads_here, HD)
    lookup_rows = selected[:, :, 0]
    content_rows = selected[:, :, 1]
    key_mask = jnp.repeat(live_slot, BLK, axis=1)[:, None, None, :]
    grad_blocks = d_out.reshape(resident_tiles, BLK, heads_here, HD)
    scores = (
        jnp.einsum("iqhd,ikhd->ihqk", query_blocks, lookup_rows, preferred_element_type=jnp.float32)
        * score_scale
    )
    largest = jnp.max(jnp.where(key_mask, scores, -1e30), axis=-1, keepdims=True)
    exp_total = jnp.sum(jnp.where(key_mask, jnp.exp(scores - largest), 0.0), axis=-1, keepdims=True)
    normalized = jnp.where(key_mask, jnp.exp(scores - largest), 0.0) / exp_total
    softmax_share = normalized.astype(jnp.bfloat16)
    attended = jnp.einsum(
        "ihqk,ikhd->iqhd", softmax_share, content_rows, preferred_element_type=jnp.float32
    ).astype(jnp.bfloat16)
    row_dot = jnp.sum(grad_blocks.astype(jnp.float32) * attended.astype(jnp.float32), axis=-1)
    value_terms = jnp.einsum(
        "ihqk,iqhd->ikhd", softmax_share, grad_blocks, preferred_element_type=jnp.float32
    )
    probability_gradient = jnp.einsum(
        "iqhd,ikhd->ihqk", grad_blocks, content_rows, preferred_element_type=jnp.float32
    )
    recomputed = jnp.where(key_mask, jnp.exp(scores - largest), 0.0) / exp_total
    score_derivative = (
        recomputed * (probability_gradient - jnp.transpose(row_dot, (0, 2, 1))[:, :, :, None])
    ).astype(jnp.bfloat16)
    query_grad = (
        jnp.einsum(
            "ihqk,ikhd->iqhd", score_derivative, lookup_rows, preferred_element_type=jnp.float32
        )
        * score_scale
    )
    key_terms = (
        jnp.einsum(
            "ihqk,iqhd->ikhd", score_derivative, query_blocks, preferred_element_type=jnp.float32
        )
        * score_scale
    )
    flat_index = drop_index.reshape(-1)
    slot_owner = (flat_index[None, :] == jnp.arange(extent, dtype=jnp.int32)[:, None]).astype(
        jnp.float32
    )
    slot_terms = jnp.concatenate(
        [
            key_terms.reshape(resident_tiles * slots, BLK, local_width),
            value_terms.reshape(resident_tiles * slots, BLK, local_width),
        ],
        axis=2,
    )
    pair_grads = jnp.einsum(
        "es,sbc->ebc",
        slot_owner,
        slot_terms,
        precision=lax.Precision.HIGHEST,
        preferred_element_type=jnp.float32,
    )
    grad_total = rounded_terms(pair_grads[own_start : own_start + resident_tiles])
    for offset in range(1, OMAX + 1):
        for direction in (1, -1):
            domain_first_index = own_start + direction * offset * resident_tiles
            region = pair_grads[domain_first_index : domain_first_index + resident_tiles]
            arrived = shifted(region.astype(jnp.bfloat16), "ctx", direction * offset).astype(
                jnp.float32
            )
            grad_total = grad_total + arrived
    attended_all = attended.reshape(tok_rows, local_width)
    query_all = query_grad.reshape(tok_rows, local_width)
    grad_projected = jnp.concatenate(
        [query_all, grad_total.reshape(tok_rows, 2 * local_width)], axis=1
    ).astype(jnp.bfloat16)
    partial_sum = jnp.einsum(
        "tc,dc->td", grad_projected, w_flat, preferred_element_type=jnp.float32
    )
    grad_features = lax.psum_scatter(
        partial_sum.astype(jnp.bfloat16), "head", scatter_dimension=1, tiled=True
    )
    return (attended_all, grad_features)


def solution(mesh):
    return jax.shard_map(
        body,
        mesh=mesh,
        in_specs=(P("ctx", "head"), P(None, None, "head"), P("ctx", None), P("ctx", "head")),
        out_specs=(P("ctx", "head"), P("ctx", "head")),
        check_vma=False,
    )
```

profile of v0, /device:TPU:8, one launch (start us, length us, event | category | flops | bytes accessed | tf_op | source)
XLA Modules:
  0.0 183.2 jit_solution(3778253173048944143)
XLA Ops:
  7.2 13.3 %all_gather.3 = bf16[256,1024]{1,0:T(8,128)(2,1)S(1)} all-gather(bf16[256,256]{1,0:T(8,128)(2,1)} %param.4), channel_id=1, replica_groups=mesh['ctx'=128,'head'=4] {'head'}, dimensions={1}, use_global_device_ids=true | all-gather | bytes 655360 | tf_op jit(solution)/shard_map/all_gather | solution.py:30
  20.6 1.7 copy.33
  24.3 7.4 %collective-permute-start.4 = (bf16[2,128,512]{2,1,0:T(8,128)(2,1)S(1)}, bf16[2,128,512]{2,1,0:T(8,128)(2,1)S(1)}, u32[]{:S(2)}, u32[]{:S(2)}) collective-permute-start(bf16[2,128,512]{2,1,0:T(8,128)(2,1)S(1)} %bitcast.63), channel_id=1, source_target_pairs={{8,0},{12,4},{16,8},{20,12},{24,16},{28,20},{32,24},{36,28},{40,32... | collective-permute-start | bytes 786440 | tf_op jit(solution)/shard_map/ppermute | solution.py:14
  31.6 2.7 %collective-permute-start.2 = (bf16[2,128,512]{2,1,0:T(8,128)(2,1)S(1)}, bf16[2,128,512]{2,1,0:T(8,128)(2,1)S(1)}, u32[]{:S(2)}, u32[]{:S(2)}) collective-permute-start(bf16[2,128,512]{2,1,0:T(8,128)(2,1)S(1)} %bitcast.64), channel_id=1, source_target_pairs={{0,4},{4,8},{8,12},{12,16},{16,20},{20,24},{24,28},{28,32},{32,36}... | collective-permute-start | bytes 786440 | tf_op jit(solution)/shard_map/ppermute | solution.py:14
  34.3 3.6 %collective-permute-start.1 = (bf16[2,128,512]{2,1,0:T(8,128)(2,1)S(1)}, bf16[2,128,512]{2,1,0:T(8,128)(2,1)}, u32[]{:S(2)}, u32[]{:S(2)}) collective-permute-start(bf16[2,128,512]{2,1,0:T(8,128)(2,1)S(1)} %bitcast.65), channel_id=1, source_target_pairs={{0,8},{4,12},{8,16},{12,20},{16,24},{20,28},{24,32},{28,36},{32,40... | collective-permute-start | bytes 786440 | tf_op jit(solution)/shard_map/ppermute | solution.py:14
  38.0 2.3 %collective-permute-start = (bf16[2,128,512]{2,1,0:T(8,128)(2,1)S(1)}, bf16[2,128,512]{2,1,0:T(8,128)(2,1)}, u32[]{:S(2)}, u32[]{:S(2)}) collective-permute-start(bf16[2,128,512]{2,1,0:T(8,128)(2,1)S(1)} %bitcast.66), channel_id=1, source_target_pairs={{0,12},{4,16},{8,20},{12,24},{16,28},{20,32},{24,36},{28,40},{32,4... | collective-permute-start | bytes 786440 | tf_op jit(solution)/shard_map/ppermute | solution.py:14
  40.9 11.3 %collective-permute-done = bf16[2,128,512]{2,1,0:T(8,128)(2,1)} collective-permute-done((bf16[2,128,512]{2,1,0:T(8,128)(2,1)S(1)}, bf16[2,128,512]{2,1,0:T(8,128)(2,1)}, u32[]{:S(2)}, u32[]{:S(2)}) %collective-permute-start) | collective-permute-done | bytes 262176 | tf_op jit(solution)/shard_map/ppermute | solution.py:14
  52.1 1.9 %collective-permute-start.3 = (bf16[2,128,512]{2,1,0:T(8,128)(2,1)S(1)}, bf16[2,128,512]{2,1,0:T(8,128)(2,1)S(1)}, u32[]{:S(2)}, u32[]{:S(2)}) collective-permute-start(bf16[2,128,512]{2,1,0:T(8,128)(2,1)S(1)} %bitcast.67), channel_id=1, source_target_pairs={{4,0},{8,4},{12,8},{16,12},{20,16},{24,20},{28,24},{32,28},{36,32}... | collective-permute-start | bytes 786440 | tf_op jit(solution)/shard_map/ppermute | solution.py:14
  54.1 1.7 constant_dynamic-update-slice_fusion.6
  55.7 1.7 constant_dynamic-update-slice_fusion.5
  61.0 2.2 %gather_fusion = bf16[18,128,512]{2,1,0:T(8,128)(2,1)S(1)} fusion(bf16[14,128,512]{2,1,0:T(8,128)(2,1)} %constant_dynamic-update-slice_fusion, s32[1024]{0:T(1024)S(1)} %pad_clamp_fusion), kind=kCustom, calls=%fused_computation | custom fusion | bytes 4718664 | tf_op jit(solution)/shard_map/gather | solution.py:56
  63.2 2.3 %reshape.43 = bf16[2,1152,2,2,128]{4,3,2,1,0:T(2,128)(2,1)} reshape(bf16[18,128,512]{2,1,0:T(8,128)(2,1)S(1)} %gather_fusion) | data formatting | bytes 4718592 | tf_op jit(solution)/shard_map/reshape | solution.py:56
  65.6 2.9 %fusion.42 = (bf16[2,1152,1,2,128]{4,3,2,1,0:T(2,128)(2,1)S(1)}, bf16[2,1152,1,2,128]{4,3,2,1,0:T(2,128)(2,1)S(1)}) fusion(bf16[2,1152,2,2,128]{4,3,2,1,0:T(2,128)(2,1)} %reshape.43), kind=kLoop, calls=%fused_computation.61 | loop fusion | bytes 4718592 | tf_op jit(solution)/shard_map/slice | solution.py:57
  68.5 2.8 %copy.56 = bf16[2,1152,1,2,128]{1,4,3,0,2:T(8,128)(2,1)} copy(bf16[2,1152,1,2,128]{4,3,2,1,0:T(2,128)(2,1)S(1)} %get-tuple-element.3) | data formatting | bytes 2359296
  75.2 1.6 fusion.16
  76.9 8.9 %copy.48 = f32[2,1152,2,128]{3,2,1,0:T(2,128)S(1)} copy(f32[2,1152,2,128]{3,1,2,0:T(8,128)S(1)} %convolution_bitcast_fusion) | data formatting | bytes 4718592 | tf_op jit(solution)/shard_map/ihqk,iqhd->ikhd/transpose | solution.py:73
  85.8 2.9 %reshape.49 = f32[18,128,256]{2,1,0:T(8,128)} reshape(f32[2,1152,2,128]{3,2,1,0:T(2,128)S(1)} %copy.48) | data formatting | bytes 4718592 | tf_op jit(solution)/shard_map/reshape | solution.py:102
  88.7 3.2 %copy.50 = f32[18,128,256]{2,0,1:T(8,128)S(1)} copy(f32[18,128,256]{2,1,0:T(8,128)} %reshape.49) | data formatting | bytes 4718592 | tf_op jit(solution)/shard_map/reshape | solution.py:102
  91.9 1.9 %fusion.13 = f32[2,1152,2,128]{1,3,2,0:T(8,128)} fusion(bf16[2,128,2,128]{1,3,2,0:T(8,128)(2,1)S(1)} %copy.44, bf16[2,2,128,1152]{3,2,1,0:T(8,128)(2,1)S(1)} %copy-done.4), kind=kOutput, calls=%fused_computation.15 | convolution fusion | flops 151584768 | bytes 3670016 | tf_op jit(solution)/shard_map/ihqk,iqhd->ikhd/dot_general | solution.py:90
  93.8 5.0 %copy.45 = f32[2,1152,2,128]{3,2,1,0:T(2,128)} copy(f32[2,1152,2,128]{1,3,2,0:T(8,128)} %fusion.13) | data formatting | bytes 4718592 | tf_op jit(solution)/shard_map/mul | solution.py:90
  98.7 4.1 %reshape.48 = f32[18,128,256]{2,1,0:T(8,128)} reshape(f32[2,1152,2,128]{3,2,1,0:T(2,128)} %copy.45) | data formatting | bytes 4718592 | tf_op jit(solution)/shard_map/reshape | solution.py:101
  102.9 3.1 %copy.49 = f32[18,128,256]{2,0,1:T(8,128)S(1)} copy(f32[18,128,256]{2,1,0:T(8,128)} %reshape.48) | data formatting | bytes 4718592 | tf_op jit(solution)/shard_map/reshape | solution.py:101
  106.0 3.7 %fusion.1 = bf16[14,128,512]{2,0,1:T(8,128)(2,1)S(1)} fusion(f32[18,128,256]{2,0,1:T(8,128)S(1)} %copy.50, f32[18,128,256]{2,0,1:T(8,128)S(1)} %copy.49, s32[18]{0:T(128)S(1)} %eq.15), kind=kOutput, calls=%fused_computation.2 | convolution fusion | flops 199360768 | bytes 6553672 | tf_op jit(solution)/shard_map/es,sbc->ebc/dot_general | solution.py:106
  112.3 6.3 %collective-permute-start.10 = (bf16[2,128,512]{2,1,0:T(8,128)(2,1)S(1)}, bf16[2,128,512]{2,1,0:T(8,128)(2,1)}, u32[]{:S(2)}, u32[]{:S(2)}) collective-permute-start(bf16[2,128,512]{2,1,0:T(8,128)(2,1)S(1)} %get-tuple-element.6), channel_id=1, source_target_pairs={{0,12},{4,16},{8,20},{12,24},{16,28},{20,32},{24,36},{28,40},{32,4... | collective-permute-start | bytes 786440 | tf_op jit(solution)/shard_map/ppermute | solution.py:14
  118.6 2.6 %collective-permute-start.9 = (bf16[2,128,512]{2,1,0:T(8,128)(2,1)S(1)}, bf16[2,128,512]{2,1,0:T(8,128)(2,1)}, u32[]{:S(2)}, u32[]{:S(2)}) collective-permute-start(bf16[2,128,512]{2,1,0:T(8,128)(2,1)S(1)} %get-tuple-element.7), channel_id=1, source_target_pairs={{8,0},{12,4},{16,8},{20,12},{24,16},{28,20},{32,24},{36,28},{40,32... | collective-permute-start | bytes 786440 | tf_op jit(solution)/shard_map/ppermute | solution.py:14
  121.3 3.2 %collective-permute-start.8 = (bf16[2,128,512]{2,1,0:T(8,128)(2,1)S(1)}, bf16[2,128,512]{2,1,0:T(8,128)(2,1)}, u32[]{:S(2)}, u32[]{:S(2)}) collective-permute-start(bf16[2,128,512]{2,1,0:T(8,128)(2,1)S(1)} %get-tuple-element.8), channel_id=1, source_target_pairs={{0,8},{4,12},{8,16},{12,20},{16,24},{20,28},{24,32},{28,36},{32,40... | collective-permute-start | bytes 786440 | tf_op jit(solution)/shard_map/ppermute | solution.py:14
  124.5 3.0 %collective-permute-start.7 = (bf16[2,128,512]{2,1,0:T(8,128)(2,1)S(1)}, bf16[2,128,512]{2,1,0:T(8,128)(2,1)}, u32[]{:S(2)}, u32[]{:S(2)}) collective-permute-start(bf16[2,128,512]{2,1,0:T(8,128)(2,1)S(1)} %get-tuple-element.9), channel_id=1, source_target_pairs={{4,0},{8,4},{12,8},{16,12},{20,16},{24,20},{28,24},{32,28},{36,32}... | collective-permute-start | bytes 786440 | tf_op jit(solution)/shard_map/ppermute | solution.py:14
  127.5 2.1 %collective-permute-start.6 = (bf16[2,128,512]{2,1,0:T(8,128)(2,1)S(1)}, bf16[2,128,512]{2,1,0:T(8,128)(2,1)}, u32[]{:S(2)}, u32[]{:S(2)}) collective-permute-start(bf16[2,128,512]{2,1,0:T(8,128)(2,1)S(1)} %get-tuple-element.10), channel_id=1, source_target_pairs={{0,4},{4,8},{8,12},{12,16},{16,20},{20,24},{24,28},{28,32},{32,36}... | collective-permute-start | bytes 786440 | tf_op jit(solution)/shard_map/ppermute | solution.py:14
  132.1 2.8 %collective-permute-done.8 = bf16[2,128,512]{2,1,0:T(8,128)(2,1)} collective-permute-done((bf16[2,128,512]{2,1,0:T(8,128)(2,1)S(1)}, bf16[2,128,512]{2,1,0:T(8,128)(2,1)}, u32[]{:S(2)}, u32[]{:S(2)}) %collective-permute-start.8) | collective-permute-done | bytes 262176 | tf_op jit(solution)/shard_map/ppermute | solution.py:14
  134.9 2.4 %collective-permute-done.6 = bf16[2,128,512]{2,1,0:T(8,128)(2,1)} collective-permute-done((bf16[2,128,512]{2,1,0:T(8,128)(2,1)S(1)}, bf16[2,128,512]{2,1,0:T(8,128)(2,1)}, u32[]{:S(2)}, u32[]{:S(2)}) %collective-permute-start.6) | collective-permute-done | bytes 262176 | tf_op jit(solution)/shard_map/ppermute | solution.py:14
  137.3 1.5 add_convert_fusion
  141.1 35.3 %reduce-scatter.2.cloned.1.call-done = bf16[256,256]{1,0:T(8,128)(2,1)} async-done(((bf16[256,1024]{1,0:T(8,128)(2,1)}), bf16[256,256]{1,0:T(8,128)(2,1)}) %reduce-scatter.2.cloned.1.call-update) | async-done | bytes 131088 | tf_op jit(solution)/shard_map/reduce_scatter | solution.py:130
  (64 shorter events, 17.3 us)
Async XLA Ops:
  7.2 169.2 %reduce-scatter.2.cloned.1.call-start = ((), (), s32[]{:S(2)}) async-start(), calls=%async_computation.1 | async-start | bytes 655360 | tf_op jit(solution)/shard_map/reduce_scatter | solution.py:130
  22.3 18.3 %copy-start.2 = (bf16[1024,3,256]{0,2,1:T(8,128)(2,1)}, bf16[1024,3,256]{0,2,1:T(8,128)(2,1)S(1)}, u32[]{:S(2)}) copy-start(bf16[1024,3,256]{0,2,1:T(8,128)(2,1)S(1)} %copy.33) | copy-start | bytes 4718596
  22.3 17.9 %copy-start.9 = (s32[2,9]{1,0:T(2,128)S(1)}, s32[2,9]{1,0:T(2,128)}, u32[]{:S(2)}) copy-start(s32[2,9]{1,0:T(2,128)} %param.6) | copy-start | bytes 220
  22.3 18.2 %copy-start.7 = (bf16[256,256]{1,0:T(8,128)(2,1)S(1)}, bf16[256,256]{1,0:T(8,128)(2,1)}, u32[]{:S(2)}) copy-start(bf16[256,256]{1,0:T(8,128)(2,1)} %param.7) | copy-start | bytes 393220
  23.0 37.3 %collective-permute-start.5 = (bf16[2,128,512]{2,1,0:T(8,128)(2,1)S(1)}, bf16[2,128,512]{2,1,0:T(8,128)(2,1)S(1)}, u32[]{:S(2)}, u32[]{:S(2)}) collective-permute-start(bf16[2,128,512]{2,1,0:T(8,128)(2,1)S(1)} %bitcast.62), channel_id=1, source_target_pairs={{12,0},{16,4},{20,8},{24,12},{28,16},{32,20},{36,24},{40,28},{44,3... | collective-permute-start | bytes 786440 | tf_op jit(solution)/shard_map/ppermute | solution.py:14
  24.3 35.3 %collective-permute-start.4 = (bf16[2,128,512]{2,1,0:T(8,128)(2,1)S(1)}, bf16[2,128,512]{2,1,0:T(8,128)(2,1)S(1)}, u32[]{:S(2)}, u32[]{:S(2)}) collective-permute-start(bf16[2,128,512]{2,1,0:T(8,128)(2,1)S(1)} %bitcast.63), channel_id=1, source_target_pairs={{8,0},{12,4},{16,8},{20,12},{24,16},{28,20},{32,24},{36,28},{40,32... | collective-permute-start | bytes 786440 | tf_op jit(solution)/shard_map/ppermute | solution.py:14
  31.6 25.8 %collective-permute-start.2 = (bf16[2,128,512]{2,1,0:T(8,128)(2,1)S(1)}, bf16[2,128,512]{2,1,0:T(8,128)(2,1)S(1)}, u32[]{:S(2)}, u32[]{:S(2)}) collective-permute-start(bf16[2,128,512]{2,1,0:T(8,128)(2,1)S(1)} %bitcast.64), channel_id=1, source_target_pairs={{0,4},{4,8},{8,12},{12,16},{16,20},{20,24},{24,28},{28,32},{32,36}... | collective-permute-start | bytes 786440 | tf_op jit(solution)/shard_map/ppermute | solution.py:14
  34.3 21.4 %collective-permute-start.1 = (bf16[2,128,512]{2,1,0:T(8,128)(2,1)S(1)}, bf16[2,128,512]{2,1,0:T(8,128)(2,1)}, u32[]{:S(2)}, u32[]{:S(2)}) collective-permute-start(bf16[2,128,512]{2,1,0:T(8,128)(2,1)S(1)} %bitcast.65), channel_id=1, source_target_pairs={{0,8},{4,12},{8,16},{12,20},{16,24},{20,28},{24,32},{28,36},{32,40... | collective-permute-start | bytes 786440 | tf_op jit(solution)/shard_map/ppermute | solution.py:14
  38.0 14.2 %collective-permute-start = (bf16[2,128,512]{2,1,0:T(8,128)(2,1)S(1)}, bf16[2,128,512]{2,1,0:T(8,128)(2,1)}, u32[]{:S(2)}, u32[]{:S(2)}) collective-permute-start(bf16[2,128,512]{2,1,0:T(8,128)(2,1)S(1)} %bitcast.66), channel_id=1, source_target_pairs={{0,12},{4,16},{8,20},{12,24},{16,28},{20,32},{24,36},{28,40},{32,4... | collective-permute-start | bytes 786440 | tf_op jit(solution)/shard_map/ppermute | solution.py:14
  52.1 6.7 %collective-permute-start.3 = (bf16[2,128,512]{2,1,0:T(8,128)(2,1)S(1)}, bf16[2,128,512]{2,1,0:T(8,128)(2,1)S(1)}, u32[]{:S(2)}, u32[]{:S(2)}) collective-permute-start(bf16[2,128,512]{2,1,0:T(8,128)(2,1)S(1)} %bitcast.67), channel_id=1, source_target_pairs={{4,0},{8,4},{12,8},{16,12},{20,16},{24,20},{28,24},{32,28},{36,32}... | collective-permute-start | bytes 786440 | tf_op jit(solution)/shard_map/ppermute | solution.py:14
  68.5 3.4 %copy-start = (bf16[2,1152,1,2,128]{4,3,2,1,0:T(2,128)(2,1)}, bf16[2,1152,1,2,128]{4,3,2,1,0:T(2,128)(2,1)S(1)}, u32[]{:S(2)}) copy-start(bf16[2,1152,1,2,128]{4,3,2,1,0:T(2,128)(2,1)S(1)} %get-tuple-element.2) | copy-start | bytes 3538948
  72.7 1.3 copy-start.6
  88.7 3.2 %copy-start.4 = (bf16[2,2,128,1152]{3,2,1,0:T(8,128)(2,1)S(1)}, bf16[2,2,128,1152]{3,2,1,0:T(8,128)(2,1)}, u32[]{:S(2)}) copy-start(bf16[2,2,128,1152]{3,2,1,0:T(8,128)(2,1)} %fusion.16) | copy-start | bytes 3538948
  110.7 18.9 %copy-start.1 = (bf16[2,1152,1,2,128]{4,3,2,1,0:T(2,128)(2,1)S(1)}, bf16[2,1152,1,2,128]{4,3,2,1,0:T(2,128)(2,1)}, u32[]{:S(2)}) copy-start(bf16[2,1152,1,2,128]{4,3,2,1,0:T(2,128)(2,1)} %copy-done) | copy-start | bytes 3538948
  110.7 18.9 %copy-start.5 = (bf16[2,2,128,1152]{3,2,1,0:T(8,128)(2,1)S(1)}, bf16[2,2,128,1152]{3,2,1,0:T(8,128)(2,1)}, u32[]{:S(2)}) copy-start(bf16[2,2,128,1152]{3,2,1,0:T(8,128)(2,1)} %fusion.16) | copy-start | bytes 3538948
  110.9 16.6 %collective-permute-start.11 = (bf16[2,128,512]{2,1,0:T(8,128)(2,1)S(1)}, bf16[2,128,512]{2,1,0:T(8,128)(2,1)S(1)}, u32[]{:S(2)}, u32[]{:S(2)}) collective-permute-start(bf16[2,128,512]{2,1,0:T(8,128)(2,1)S(1)} %get-tuple-element.5), channel_id=1, source_target_pairs={{12,0},{16,4},{20,8},{24,12},{28,16},{32,20},{36,24},{40,28},{44,3... | collective-permute-start | bytes 786440 | tf_op jit(solution)/shard_map/ppermute | solution.py:14
  112.3 19.7 %collective-permute-start.10 = (bf16[2,128,512]{2,1,0:T(8,128)(2,1)S(1)}, bf16[2,128,512]{2,1,0:T(8,128)(2,1)}, u32[]{:S(2)}, u32[]{:S(2)}) collective-permute-start(bf16[2,128,512]{2,1,0:T(8,128)(2,1)S(1)} %get-tuple-element.6), channel_id=1, source_target_pairs={{0,12},{4,16},{8,20},{12,24},{16,28},{20,32},{24,36},{28,40},{32,4... | collective-permute-start | bytes 786440 | tf_op jit(solution)/shard_map/ppermute | solution.py:14
  118.6 13.4 %collective-permute-start.9 = (bf16[2,128,512]{2,1,0:T(8,128)(2,1)S(1)}, bf16[2,128,512]{2,1,0:T(8,128)(2,1)}, u32[]{:S(2)}, u32[]{:S(2)}) collective-permute-start(bf16[2,128,512]{2,1,0:T(8,128)(2,1)S(1)} %get-tuple-element.7), channel_id=1, source_target_pairs={{8,0},{12,4},{16,8},{20,12},{24,16},{28,20},{32,24},{36,28},{40,32... | collective-permute-start | bytes 786440 | tf_op jit(solution)/shard_map/ppermute | solution.py:14
  121.3 13.6 %collective-permute-start.8 = (bf16[2,128,512]{2,1,0:T(8,128)(2,1)S(1)}, bf16[2,128,512]{2,1,0:T(8,128)(2,1)}, u32[]{:S(2)}, u32[]{:S(2)}) collective-permute-start(bf16[2,128,512]{2,1,0:T(8,128)(2,1)S(1)} %get-tuple-element.8), channel_id=1, source_target_pairs={{0,8},{4,12},{8,16},{12,20},{16,24},{20,28},{24,32},{28,36},{32,40... | collective-permute-start | bytes 786440 | tf_op jit(solution)/shard_map/ppermute | solution.py:14
  124.5 10.4 %collective-permute-start.7 = (bf16[2,128,512]{2,1,0:T(8,128)(2,1)S(1)}, bf16[2,128,512]{2,1,0:T(8,128)(2,1)}, u32[]{:S(2)}, u32[]{:S(2)}) collective-permute-start(bf16[2,128,512]{2,1,0:T(8,128)(2,1)S(1)} %get-tuple-element.9), channel_id=1, source_target_pairs={{4,0},{8,4},{12,8},{16,12},{20,16},{24,20},{28,24},{32,28},{36,32}... | collective-permute-start | bytes 786440 | tf_op jit(solution)/shard_map/ppermute | solution.py:14
  127.5 9.8 %collective-permute-start.6 = (bf16[2,128,512]{2,1,0:T(8,128)(2,1)S(1)}, bf16[2,128,512]{2,1,0:T(8,128)(2,1)}, u32[]{:S(2)}, u32[]{:S(2)}) collective-permute-start(bf16[2,128,512]{2,1,0:T(8,128)(2,1)S(1)} %get-tuple-element.10), channel_id=1, source_target_pairs={{0,4},{4,8},{8,12},{12,16},{16,20},{20,24},{24,28},{28,32},{32,36}... | collective-permute-start | bytes 786440 | tf_op jit(solution)/shard_map/ppermute | solution.py:14
  130.9 8.0 %copy-start.3 = (bf16[1024,3,256]{0,2,1:T(8,128)(2,1)S(1)}, bf16[1024,3,256]{0,2,1:T(8,128)(2,1)}, u32[]{:S(2)}) copy-start(bf16[1024,3,256]{0,2,1:T(8,128)(2,1)} %copy-done.2) | copy-start | bytes 4718596
  138.8 1.4 copy-start.8
Sparse Core Ops, SparseCore 0:
  140.3 36.0 reduce-scatter.1
where the time goes:
time: 184 us; the launch traced here: 183 us
  waiting for transfers between devices  51.9 us (28%)
  local copies, waits for them, and re-layouts  50.5 us (27%)
  starting transfers between devices  37.8 us (21%)
  between operations  14.4 us (8%)
  blocking collectives  13.3 us (7%)
  matrix products  13 us (7%)
  other arithmetic  2.32 us (1%)
    ppermute x12, starting transfers between devices, shifted(): lax.ppermute(value, axis, [(source, source + steps) for source in range(f...  37.7 us
    reduce_scatter x1, waiting for transfers between devices, body(): lax.psum_scatter(partial_sum.astype(jnp.bfloat16), 'head', scatter_dimens...  35.3 us
    ppermute x12, waiting for transfers between devices, shifted(): lax.ppermute(value, axis, [(source, source + steps) for source in range(f...  16.5 us
    all_gather x1, blocking collectives, body(): lax.all_gather(features, 'head', axis=1, tiled=True)  13.3 us
    unnamed x32, local copies, waits for them, and re-layouts  12.1 us
    transpose x1, local copies, waits for them, and re-layouts, body(): jnp.einsum('ihqk,iqhd->ikhd', softmax_share, grad_blocks, preferred_eleme...  8.88 us
    reshape x2, local copies, waits for them, and re-layouts, body(): key_terms.reshape(resident_tiles * slots, BLK, local_width)  7.22 us
    reshape x2, local copies, waits for them, and re-layouts, body(): value_terms.reshape(resident_tiles * slots, BLK, local_width)  6.11 us
  transfers between devices with their start and end apart: 13, of which 4 were waited for; matrix products, arithmetic and copies ran while one was open for 5% of the time, Pallas kernels for 0%

commit v1 on v0

--- a/solution.py
+++ b/solution.py
@@ -6,6 +6,29 @@
 HD = 128
 BLK = 128
 OMAX = 3
+
+
+def show_case(sample, row_axis):
+    piece_next, z1, z = (jax.lax.axis_size(row_axis), jax.lax.axis_index(row_axis), sample.shape[1])
+    by_rank = []
+    for no in range(piece_next):
+        by_rank.append((no, (no + 1) % piece_next))
+    panels = []
+    for no in range(piece_next):
+        panels.append((no, (no - 1) % piece_next))
+    x_now = jnp.zeros((*sample.shape[:1], piece_next * z, *sample.shape[2:]), sample.dtype)
+    step_out = placed = sample
+    x_now = lax.dynamic_update_slice_in_dim(x_now, sample, z1 * z, axis=1)
+    lower = piece_next // 2
+    for s in range(1, lower + 1):
+        step_out = jax.lax.ppermute(step_out, row_axis, by_rank)
+        x_now = lax.dynamic_update_slice_in_dim(x_now, step_out, (z1 - s) % piece_next * z, axis=1)
+        if s < piece_next - lower:
+            placed = jax.lax.ppermute(placed, row_axis, panels)
+            x_now = lax.dynamic_update_slice_in_dim(
+                x_now, placed, (z1 + s) % piece_next * z, axis=1
+            )
+    return x_now
 
 
 def shifted(value, axis, steps):
@@ -26,11 +49,7 @@
     heads_here = local_width // HD
     score_scale = HD ** (-0.5)
     w_flat = w_qkv.reshape(model_width, 3 * local_width)
-    projected = jnp.dot(
-        lax.all_gather(features, "head", axis=1, tiled=True),
-        w_flat,
-        preferred_element_type=jnp.float32,
-    )
+    projected = jnp.dot(show_case(features, "head"), w_flat, preferred_element_type=jnp.float32)
     projected = projected.astype(jnp.bfloat16)
     query_blocks = projected[:, :local_width].reshape(resident_tiles, BLK, heads_here, HD)
     pair_blocks = projected[:, local_width:].reshape(resident_tiles, BLK, 2 * local_width)

time: 184 us -> 186 us (1.011)
  blocking collectives: 13.3 us -> 0 us
  starting transfers between devices: 37.8 us -> 45.6 us
  waiting for transfers between devices: 51.9 us -> 59 us
    all_gather x1 -> x0, blocking collectives: 13.3 us -> none  [body(): lax.all_gather(features, 'head', axis=1, tiled=True)]
    ppermute x0 -> x3, waiting for transfers between devices: none -> 8.86 us  [the longest x2 8.86 us: show_case(): step_out = jax.lax.ppermute(step_out, row_axis, by_rank)]
    ppermute x0 -> x3, starting transfers between devices: none -> 8.5 us  [the longest x1 4.67 us: show_case(): placed = jax.lax.ppermute(placed, row_axis, panels)]
    ppermute x12, waiting for transfers between devices: 16.5 us -> 13.8 us  [shifted(): lax.ppermute(value, axis, [(source, source + steps) for source in range(f...]
    unnamed x32, local copies, waits for them, and re-layouts: 12.1 us -> 10.2 us
  transfers between devices with their start and end apart: 13 -> 16, of which waited for: 4 -> 8; matrix products, arithmetic and copies ran while one was open for 5% -> 6% of each run, Pallas kernels for 0% -> 0%
where the time goes in v1:
time: 186 us; the launch traced here: 185 us
  waiting for transfers between devices  59 us (32%)
  local copies, waits for them, and re-layouts  49.5 us (27%)
  starting transfers between devices  45.6 us (25%)
  between operations  14.6 us (8%)
  matrix products  13.1 us (7%)
  other arithmetic  3 us (2%)
    ppermute x12, starting transfers between devices, shifted(): lax.ppermute(value, axis, [(source, source + steps) for source in range(f...  37 us
    reduce_scatter x1, waiting for transfers between devices, body(): lax.psum_scatter(partial_sum.astype(jnp.bfloat16), 'head', scatter_dimens...  36.3 us
    ppermute x12, waiting for transfers between devices, shifted(): lax.ppermute(value, axis, [(source, source + steps) for source in range(f...  13.8 us
    unnamed x32, local copies, waits for them, and re-layouts  10.2 us
    transpose x1, local copies, waits for them, and re-layouts, body(): jnp.einsum('ihqk,iqhd->ikhd', softmax_share, grad_blocks, preferred_eleme...  8.88 us
    ppermute x2, waiting for transfers between devices, show_case(): step_out = jax.lax.ppermute(step_out, row_axis, by_rank)  8.86 us
    reshape x2, local copies, waits for them, and re-layouts, body(): key_terms.reshape(resident_tiles * slots, BLK, local_width)  7.24 us
    reshape x2, local copies, waits for them, and re-layouts, body(): value_terms.reshape(resident_tiles * slots, BLK, local_width)  6.11 us
  transfers between devices with their start and end apart: 16, of which 8 were waited for; matrix products, arithmetic and copies ran while one was open for 6% of the time, Pallas kernels for 0%

profile of v1, /device:TPU:8, one launch (start us, length us, event | category | flops | bytes accessed | tf_op | source)
XLA Modules:
  0.0 184.7 jit_solution(9107496813521246870)
XLA Ops:
  7.2 4.7 %collective-permute-start.1 = (bf16[256,256]{1,0:T(8,128)(2,1)}, bf16[256,256]{1,0:T(8,128)(2,1)S(1)}, u32[]{:S(2)}, u32[]{:S(2)}) collective-permute-start(bf16[256,256]{1,0:T(8,128)(2,1)} %param.4), channel_id=1, source_target_pairs={{0,3},{1,0},{2,1},{3,2},{4,7},{5,4},{6,5},{7,6},{8,11},{9,8},{10,9... | collective-permute-start | bytes 393224 | tf_op jit(solution)/shard_map/ppermute | solution.py:27
  11.9 1.9 %collective-permute-start = (bf16[256,256]{1,0:T(8,128)(2,1)}, bf16[256,256]{1,0:T(8,128)(2,1)S(1)}, u32[]{:S(2)}, u32[]{:S(2)}) collective-permute-start(bf16[256,256]{1,0:T(8,128)(2,1)} %param.4), channel_id=1, source_target_pairs={{0,1},{1,2},{2,3},{3,0},{4,5},{5,6},{6,7},{7,4},{8,9},{9,10},{10,1... | collective-permute-start | bytes 393224 | tf_op jit(solution)/shard_map/ppermute | solution.py:24
  15.6 1.7 copy.33
  17.4 2.8 %collective-permute-done = bf16[256,256]{1,0:T(8,128)(2,1)S(1)} collective-permute-done((bf16[256,256]{1,0:T(8,128)(2,1)}, bf16[256,256]{1,0:T(8,128)(2,1)S(1)}, u32[]{:S(2)}, u32[]{:S(2)}) %collective-permute-start) | collective-permute-done | bytes 131104 | tf_op jit(solution)/shard_map/ppermute | solution.py:24
  20.2 1.9 %collective-permute-start.2 = (bf16[256,256]{1,0:T(8,128)(2,1)S(1)}, bf16[256,256]{1,0:T(8,128)(2,1)S(1)}, u32[]{:S(2)}, u32[]{:S(2)}) collective-permute-start(bf16[256,256]{1,0:T(8,128)(2,1)S(1)} %collective-permute-done), channel_id=1, source_target_pairs={{0,1},{1,2},{2,3},{3,0},{4,5},{5,6},{6,7},{7,4},{8,9},{9,10},{10,1... | collective-permute-start | bytes 393224 | tf_op jit(solution)/shard_map/ppermute | solution.py:24
  22.2 6.1 %collective-permute-done.2 = bf16[256,256]{1,0:T(8,128)(2,1)S(1)} collective-permute-done((bf16[256,256]{1,0:T(8,128)(2,1)S(1)}, bf16[256,256]{1,0:T(8,128)(2,1)S(1)}, u32[]{:S(2)}, u32[]{:S(2)}) %collective-permute-start.2) | collective-permute-done | bytes 131104 | tf_op jit(solution)/shard_map/ppermute | solution.py:24
  28.9 3.5 %collective-permute-start.4 = (bf16[2,128,512]{2,1,0:T(8,128)(2,1)S(1)}, bf16[2,128,512]{2,1,0:T(8,128)(2,1)S(1)}, u32[]{:S(2)}, u32[]{:S(2)}) collective-permute-start(bf16[2,128,512]{2,1,0:T(8,128)(2,1)S(1)} %bitcast.62), channel_id=1, source_target_pairs={{0,8},{4,12},{8,16},{12,20},{16,24},{20,28},{24,32},{28,36},{32,40... | collective-permute-start | bytes 786440 | tf_op jit(solution)/shard_map/ppermute | solution.py:37
  33.8 6.4 %collective-permute-start.5 = (bf16[2,128,512]{2,1,0:T(8,128)(2,1)S(1)}, bf16[2,128,512]{2,1,0:T(8,128)(2,1)S(1)}, u32[]{:S(2)}, u32[]{:S(2)}) collective-permute-start(bf16[2,128,512]{2,1,0:T(8,128)(2,1)S(1)} %bitcast.64), channel_id=1, source_target_pairs={{0,4},{4,8},{8,12},{12,16},{16,20},{20,24},{24,28},{28,32},{32,36}... | collective-permute-start | bytes 786440 | tf_op jit(solution)/shard_map/ppermute | solution.py:37
  41.8 1.9 %collective-permute-start.7 = (bf16[2,128,512]{2,1,0:T(8,128)(2,1)S(1)}, bf16[2,128,512]{2,1,0:T(8,128)(2,1)S(1)}, u32[]{:S(2)}, u32[]{:S(2)}) collective-permute-start(bf16[2,128,512]{2,1,0:T(8,128)(2,1)S(1)} %bitcast.66), channel_id=1, source_target_pairs={{8,0},{12,4},{16,8},{20,12},{24,16},{28,20},{32,24},{36,28},{40,32... | collective-permute-start | bytes 786440 | tf_op jit(solution)/shard_map/ppermute | solution.py:37
  44.0 1.9 %collective-permute-start.6 = (bf16[2,128,512]{2,1,0:T(8,128)(2,1)S(1)}, bf16[2,128,512]{2,1,0:T(8,128)(2,1)S(1)}, u32[]{:S(2)}, u32[]{:S(2)}) collective-permute-start(bf16[2,128,512]{2,1,0:T(8,128)(2,1)S(1)} %bitcast.67), channel_id=1, source_target_pairs={{4,0},{8,4},{12,8},{16,12},{20,16},{24,20},{28,24},{32,28},{36,32}... | collective-permute-start | bytes 786440 | tf_op jit(solution)/shard_map/ppermute | solution.py:37
  50.3 6.6 %collective-permute-done.6 = bf16[2,128,512]{2,1,0:T(8,128)(2,1)S(1)} collective-permute-done((bf16[2,128,512]{2,1,0:T(8,128)(2,1)S(1)}, bf16[2,128,512]{2,1,0:T(8,128)(2,1)S(1)}, u32[]{:S(2)}, u32[]{:S(2)}) %collective-permute-start.6) | collective-permute-done | bytes 262176 | tf_op jit(solution)/shard_map/ppermute | solution.py:37
  59.4 2.2 %gather_fusion = bf16[18,128,512]{2,1,0:T(8,128)(2,1)S(1)} fusion(bf16[14,128,512]{2,1,0:T(8,128)(2,1)} %constant_dynamic-update-slice_fusion, s32[1024]{0:T(1024)S(1)} %pad_clamp_fusion), kind=kCustom, calls=%fused_computation | custom fusion | bytes 4718664 | tf_op jit(solution)/shard_map/gather | solution.py:75
  61.6 2.3 %reshape.43 = bf16[2,1152,2,2,128]{4,3,2,1,0:T(2,128)(2,1)} reshape(bf16[18,128,512]{2,1,0:T(8,128)(2,1)S(1)} %gather_fusion) | data formatting | bytes 4718592 | tf_op jit(solution)/shard_map/reshape | solution.py:75
  63.9 2.9 %fusion.42 = (bf16[2,1152,1,2,128]{4,3,2,1,0:T(2,128)(2,1)S(1)}, bf16[2,1152,1,2,128]{4,3,2,1,0:T(2,128)(2,1)S(1)}) fusion(bf16[2,1152,2,2,128]{4,3,2,1,0:T(2,128)(2,1)} %reshape.43), kind=kLoop, calls=%fused_computation.65 | loop fusion | bytes 4718592 | tf_op jit(solution)/shard_map/slice | solution.py:76
  66.9 2.8 %copy.56 = bf16[2,1152,1,2,128]{1,4,3,0,2:T(8,128)(2,1)} copy(bf16[2,1152,1,2,128]{4,3,2,1,0:T(2,128)(2,1)S(1)} %get-tuple-element.3) | data formatting | bytes 2359296
  73.6 1.6 fusion.16
  75.3 8.9 %copy.48 = f32[2,1152,2,128]{3,2,1,0:T(2,128)S(1)} copy(f32[2,1152,2,128]{3,1,2,0:T(8,128)S(1)} %convolution_bitcast_fusion) | data formatting | bytes 4718592 | tf_op jit(solution)/shard_map/ihqk,iqhd->ikhd/transpose | solution.py:92
  84.2 2.9 %reshape.49 = f32[18,128,256]{2,1,0:T(8,128)} reshape(f32[2,1152,2,128]{3,2,1,0:T(2,128)S(1)} %copy.48) | data formatting | bytes 4718592 | tf_op jit(solution)/shard_map/reshape | solution.py:121
  87.1 3.2 %copy.50 = f32[18,128,256]{2,0,1:T(8,128)S(1)} copy(f32[18,128,256]{2,1,0:T(8,128)} %reshape.49) | data formatting | bytes 4718592 | tf_op jit(solution)/shard_map/reshape | solution.py:121
  90.3 1.9 %fusion.13 = f32[2,1152,2,128]{1,3,2,0:T(8,128)} fusion(bf16[2,128,2,128]{1,3,2,0:T(8,128)(2,1)S(1)} %copy.44, bf16[2,2,128,1152]{3,2,1,0:T(8,128)(2,1)S(1)} %copy-done.4), kind=kOutput, calls=%fused_computation.15 | convolution fusion | flops 151584768 | bytes 3670016 | tf_op jit(solution)/shard_map/ihqk,iqhd->ikhd/dot_general | solution.py:109
  92.2 5.0 %copy.45 = f32[2,1152,2,128]{3,2,1,0:T(2,128)} copy(f32[2,1152,2,128]{1,3,2,0:T(8,128)} %fusion.13) | data formatting | bytes 4718592 | tf_op jit(solution)/shard_map/mul | solution.py:109
  97.1 4.2 %reshape.48 = f32[18,128,256]{2,1,0:T(8,128)} reshape(f32[2,1152,2,128]{3,2,1,0:T(2,128)} %copy.45) | data formatting | bytes 4718592 | tf_op jit(solution)/shard_map/reshape | solution.py:120
  101.3 3.1 %copy.49 = f32[18,128,256]{2,0,1:T(8,128)S(1)} copy(f32[18,128,256]{2,1,0:T(8,128)} %reshape.48) | data formatting | bytes 4718592 | tf_op jit(solution)/shard_map/reshape | solution.py:120
  104.4 3.7 %fusion.1 = bf16[14,128,512]{2,0,1:T(8,128)(2,1)S(1)} fusion(f32[18,128,256]{2,0,1:T(8,128)S(1)} %copy.50, f32[18,128,256]{2,0,1:T(8,128)S(1)} %copy.49, s32[18]{0:T(128)S(1)} %eq.19), kind=kOutput, calls=%fused_computation.2 | convolution fusion | flops 199360768 | bytes 6553672 | tf_op jit(solution)/shard_map/es,sbc->ebc/dot_general | solution.py:125
  110.8 8.4 %collective-permute-start.13 = (bf16[2,128,512]{2,1,0:T(8,128)(2,1)S(1)}, bf16[2,128,512]{2,1,0:T(8,128)(2,1)}, u32[]{:S(2)}, u32[]{:S(2)}) collective-permute-start(bf16[2,128,512]{2,1,0:T(8,128)(2,1)S(1)} %get-tuple-element.6), channel_id=1, source_target_pairs={{0,12},{4,16},{8,20},{12,24},{16,28},{20,32},{24,36},{28,40},{32,4... | collective-permute-start | bytes 786440 | tf_op jit(solution)/shard_map/ppermute | solution.py:37
  119.1 2.5 %collective-permute-start.12 = (bf16[2,128,512]{2,1,0:T(8,128)(2,1)S(1)}, bf16[2,128,512]{2,1,0:T(8,128)(2,1)}, u32[]{:S(2)}, u32[]{:S(2)}) collective-permute-start(bf16[2,128,512]{2,1,0:T(8,128)(2,1)S(1)} %get-tuple-element.7), channel_id=1, source_target_pairs={{8,0},{12,4},{16,8},{20,12},{24,16},{28,20},{32,24},{36,28},{40,32... | collective-permute-start | bytes 786440 | tf_op jit(solution)/shard_map/ppermute | solution.py:37
  121.6 3.3 %collective-permute-start.11 = (bf16[2,128,512]{2,1,0:T(8,128)(2,1)S(1)}, bf16[2,128,512]{2,1,0:T(8,128)(2,1)}, u32[]{:S(2)}, u32[]{:S(2)}) collective-permute-start(bf16[2,128,512]{2,1,0:T(8,128)(2,1)S(1)} %get-tuple-element.8), channel_id=1, source_target_pairs={{0,8},{4,12},{8,16},{12,20},{16,24},{20,28},{24,32},{28,36},{32,40... | collective-permute-start | bytes 786440 | tf_op jit(solution)/shard_map/ppermute | solution.py:37
  125.0 2.8 %collective-permute-start.10 = (bf16[2,128,512]{2,1,0:T(8,128)(2,1)S(1)}, bf16[2,128,512]{2,1,0:T(8,128)(2,1)}, u32[]{:S(2)}, u32[]{:S(2)}) collective-permute-start(bf16[2,128,512]{2,1,0:T(8,128)(2,1)S(1)} %get-tuple-element.9), channel_id=1, source_target_pairs={{4,0},{8,4},{12,8},{16,12},{20,16},{24,20},{28,24},{32,28},{36,32}... | collective-permute-start | bytes 786440 | tf_op jit(solution)/shard_map/ppermute | solution.py:37
  127.8 2.2 %collective-permute-start.9 = (bf16[2,128,512]{2,1,0:T(8,128)(2,1)S(1)}, bf16[2,128,512]{2,1,0:T(8,128)(2,1)}, u32[]{:S(2)}, u32[]{:S(2)}) collective-permute-start(bf16[2,128,512]{2,1,0:T(8,128)(2,1)S(1)} %get-tuple-element.10), channel_id=1, source_target_pairs={{0,4},{4,8},{8,12},{12,16},{16,20},{20,24},{24,28},{28,32},{32,36}... | collective-permute-start | bytes 786440 | tf_op jit(solution)/shard_map/ppermute | solution.py:37
  132.6 3.0 %collective-permute-done.11 = bf16[2,128,512]{2,1,0:T(8,128)(2,1)} collective-permute-done((bf16[2,128,512]{2,1,0:T(8,128)(2,1)S(1)}, bf16[2,128,512]{2,1,0:T(8,128)(2,1)}, u32[]{:S(2)}, u32[]{:S(2)}) %collective-permute-start.11) | collective-permute-done | bytes 262176 | tf_op jit(solution)/shard_map/ppermute | solution.py:37
  135.5 2.2 %collective-permute-done.9 = bf16[2,128,512]{2,1,0:T(8,128)(2,1)} collective-permute-done((bf16[2,128,512]{2,1,0:T(8,128)(2,1)S(1)}, bf16[2,128,512]{2,1,0:T(8,128)(2,1)}, u32[]{:S(2)}, u32[]{:S(2)}) %collective-permute-start.9) | collective-permute-done | bytes 262176 | tf_op jit(solution)/shard_map/ppermute | solution.py:37
  141.5 36.3 %reduce-scatter.2.cloned.1.call-done = bf16[256,256]{1,0:T(8,128)(2,1)} async-done(((bf16[256,1024]{1,0:T(8,128)(2,1)}), bf16[256,256]{1,0:T(8,128)(2,1)}) %reduce-scatter.2.cloned.1.call-update) | async-done | bytes 131088 | tf_op jit(solution)/shard_map/reduce_scatter | solution.py:149
  (74 shorter events, 25.2 us)
Async XLA Ops:
  7.2 170.7 %reduce-scatter.2.cloned.1.call-start = ((), (), s32[]{:S(2)}) async-start(), calls=%async_computation.1 | async-start | bytes 655360 | tf_op jit(solution)/shard_map/reduce_scatter | solution.py:149
  7.2 14.9 %collective-permute-start.1 = (bf16[256,256]{1,0:T(8,128)(2,1)}, bf16[256,256]{1,0:T(8,128)(2,1)S(1)}, u32[]{:S(2)}, u32[]{:S(2)}) collective-permute-start(bf16[256,256]{1,0:T(8,128)(2,1)} %param.4), channel_id=1, source_target_pairs={{0,3},{1,0},{2,1},{3,2},{4,7},{5,4},{6,5},{7,6},{8,11},{9,8},{10,9... | collective-permute-start | bytes 393224 | tf_op jit(solution)/shard_map/ppermute | solution.py:27
  11.9 8.3 %collective-permute-start = (bf16[256,256]{1,0:T(8,128)(2,1)}, bf16[256,256]{1,0:T(8,128)(2,1)S(1)}, u32[]{:S(2)}, u32[]{:S(2)}) collective-permute-start(bf16[256,256]{1,0:T(8,128)(2,1)} %param.4), channel_id=1, source_target_pairs={{0,1},{1,2},{2,3},{3,0},{4,5},{5,6},{6,7},{7,4},{8,9},{9,10},{10,1... | collective-permute-start | bytes 393224 | tf_op jit(solution)/shard_map/ppermute | solution.py:24
  17.3 11.6 %copy-start.2 = (bf16[1024,3,256]{0,2,1:T(8,128)(2,1)}, bf16[1024,3,256]{0,2,1:T(8,128)(2,1)S(1)}, u32[]{:S(2)}) copy-start(bf16[1024,3,256]{0,2,1:T(8,128)(2,1)S(1)} %copy.33) | copy-start | bytes 4718596
  20.2 8.1 %collective-permute-start.2 = (bf16[256,256]{1,0:T(8,128)(2,1)S(1)}, bf16[256,256]{1,0:T(8,128)(2,1)S(1)}, u32[]{:S(2)}, u32[]{:S(2)}) collective-permute-start(bf16[256,256]{1,0:T(8,128)(2,1)S(1)} %collective-permute-done), channel_id=1, source_target_pairs={{0,1},{1,2},{2,3},{3,0},{4,5},{5,6},{6,7},{7,4},{8,9},{9,10},{10,1... | collective-permute-start | bytes 393224 | tf_op jit(solution)/shard_map/ppermute | solution.py:24
  22.1 11.6 %copy-start.9 = (s32[2,9]{1,0:T(2,128)S(1)}, s32[2,9]{1,0:T(2,128)}, u32[]{:S(2)}) copy-start(s32[2,9]{1,0:T(2,128)} %param.6) | copy-start | bytes 220
  22.1 18.2 %copy-start.7 = (bf16[256,256]{1,0:T(8,128)(2,1)S(1)}, bf16[256,256]{1,0:T(8,128)(2,1)}, u32[]{:S(2)}) copy-start(bf16[256,256]{1,0:T(8,128)(2,1)} %param.7) | copy-start | bytes 393220
  28.9 17.7 %collective-permute-start.4 = (bf16[2,128,512]{2,1,0:T(8,128)(2,1)S(1)}, bf16[2,128,512]{2,1,0:T(8,128)(2,1)S(1)}, u32[]{:S(2)}, u32[]{:S(2)}) collective-permute-start(bf16[2,128,512]{2,1,0:T(8,128)(2,1)S(1)} %bitcast.62), channel_id=1, source_target_pairs={{0,8},{4,12},{8,16},{12,20},{16,24},{20,28},{24,32},{28,36},{32,40... | collective-permute-start | bytes 786440 | tf_op jit(solution)/shard_map/ppermute | solution.py:37
  32.4 11.5 %collective-permute-start.3 = (bf16[2,128,512]{2,1,0:T(8,128)(2,1)S(1)}, bf16[2,128,512]{2,1,0:T(8,128)(2,1)S(1)}, u32[]{:S(2)}, u32[]{:S(2)}) collective-permute-start(bf16[2,128,512]{2,1,0:T(8,128)(2,1)S(1)} %bitcast.63), channel_id=1, source_target_pairs={{0,12},{4,16},{8,20},{12,24},{16,28},{20,32},{24,36},{28,40},{32,4... | collective-permute-start | bytes 786440 | tf_op jit(solution)/shard_map/ppermute | solution.py:37
  33.8 15.0 %collective-permute-start.5 = (bf16[2,128,512]{2,1,0:T(8,128)(2,1)S(1)}, bf16[2,128,512]{2,1,0:T(8,128)(2,1)S(1)}, u32[]{:S(2)}, u32[]{:S(2)}) collective-permute-start(bf16[2,128,512]{2,1,0:T(8,128)(2,1)S(1)} %bitcast.64), channel_id=1, source_target_pairs={{0,4},{4,8},{8,12},{12,16},{16,20},{20,24},{24,28},{28,32},{32,36}... | collective-permute-start | bytes 786440 | tf_op jit(solution)/shard_map/ppermute | solution.py:37
  40.5 18.2 %collective-permute-start.8 = (bf16[2,128,512]{2,1,0:T(8,128)(2,1)S(1)}, bf16[2,128,512]{2,1,0:T(8,128)(2,1)S(1)}, u32[]{:S(2)}, u32[]{:S(2)}) collective-permute-start(bf16[2,128,512]{2,1,0:T(8,128)(2,1)S(1)} %bitcast.65), channel_id=1, source_target_pairs={{12,0},{16,4},{20,8},{24,12},{28,16},{32,20},{36,24},{40,28},{44,3... | collective-permute-start | bytes 786440 | tf_op jit(solution)/shard_map/ppermute | solution.py:37
  41.8 16.1 %collective-permute-start.7 = (bf16[2,128,512]{2,1,0:T(8,128)(2,1)S(1)}, bf16[2,128,512]{2,1,0:T(8,128)(2,1)S(1)}, u32[]{:S(2)}, u32[]{:S(2)}) collective-permute-start(bf16[2,128,512]{2,1,0:T(8,128)(2,1)S(1)} %bitcast.66), channel_id=1, source_target_pairs={{8,0},{12,4},{16,8},{20,12},{24,16},{28,20},{32,24},{36,28},{40,32... | collective-permute-start | bytes 786440 | tf_op jit(solution)/shard_map/ppermute | solution.py:37
  44.0 12.9 %collective-permute-start.6 = (bf16[2,128,512]{2,1,0:T(8,128)(2,1)S(1)}, bf16[2,128,512]{2,1,0:T(8,128)(2,1)S(1)}, u32[]{:S(2)}, u32[]{:S(2)}) collective-permute-start(bf16[2,128,512]{2,1,0:T(8,128)(2,1)S(1)} %bitcast.67), channel_id=1, source_target_pairs={{4,0},{8,4},{12,8},{16,12},{20,16},{24,20},{28,24},{32,28},{36,32}... | collective-permute-start | bytes 786440 | tf_op jit(solution)/shard_map/ppermute | solution.py:37
  66.9 3.4 %copy-start = (bf16[2,1152,1,2,128]{4,3,2,1,0:T(2,128)(2,1)}, bf16[2,1152,1,2,128]{4,3,2,1,0:T(2,128)(2,1)S(1)}, u32[]{:S(2)}) copy-start(bf16[2,1152,1,2,128]{4,3,2,1,0:T(2,128)(2,1)S(1)} %get-tuple-element.2) | copy-start | bytes 3538948
  71.1 1.3 copy-start.6
  87.1 3.2 %copy-start.4 = (bf16[2,2,128,1152]{3,2,1,0:T(8,128)(2,1)S(1)}, bf16[2,2,128,1152]{3,2,1,0:T(8,128)(2,1)}, u32[]{:S(2)}) copy-start(bf16[2,2,128,1152]{3,2,1,0:T(8,128)(2,1)} %fusion.16) | copy-start | bytes 3538948
  109.1 21.0 %copy-start.1 = (bf16[2,1152,1,2,128]{4,3,2,1,0:T(2,128)(2,1)S(1)}, bf16[2,1152,1,2,128]{4,3,2,1,0:T(2,128)(2,1)}, u32[]{:S(2)}) copy-start(bf16[2,1152,1,2,128]{4,3,2,1,0:T(2,128)(2,1)} %copy-done) | copy-start | bytes 3538948
  109.1 21.0 %copy-start.5 = (bf16[2,2,128,1152]{3,2,1,0:T(8,128)(2,1)S(1)}, bf16[2,2,128,1152]{3,2,1,0:T(8,128)(2,1)}, u32[]{:S(2)}) copy-start(bf16[2,2,128,1152]{3,2,1,0:T(8,128)(2,1)} %fusion.16) | copy-start | bytes 3538948
  109.3 18.5 %collective-permute-start.14 = (bf16[2,128,512]{2,1,0:T(8,128)(2,1)S(1)}, bf16[2,128,512]{2,1,0:T(8,128)(2,1)S(1)}, u32[]{:S(2)}, u32[]{:S(2)}) collective-permute-start(bf16[2,128,512]{2,1,0:T(8,128)(2,1)S(1)} %get-tuple-element.5), channel_id=1, source_target_pairs={{12,0},{16,4},{20,8},{24,12},{28,16},{32,20},{36,24},{40,28},{44,3... | collective-permute-start | bytes 786440 | tf_op jit(solution)/shard_map/ppermute | solution.py:37
  110.8 21.8 %collective-permute-start.13 = (bf16[2,128,512]{2,1,0:T(8,128)(2,1)S(1)}, bf16[2,128,512]{2,1,0:T(8,128)(2,1)}, u32[]{:S(2)}, u32[]{:S(2)}) collective-permute-start(bf16[2,128,512]{2,1,0:T(8,128)(2,1)S(1)} %get-tuple-element.6), channel_id=1, source_target_pairs={{0,12},{4,16},{8,20},{12,24},{16,28},{20,32},{24,36},{28,40},{32,4... | collective-permute-start | bytes 786440 | tf_op jit(solution)/shard_map/ppermute | solution.py:37
  119.1 13.4 %collective-permute-start.12 = (bf16[2,128,512]{2,1,0:T(8,128)(2,1)S(1)}, bf16[2,128,512]{2,1,0:T(8,128)(2,1)}, u32[]{:S(2)}, u32[]{:S(2)}) collective-permute-start(bf16[2,128,512]{2,1,0:T(8,128)(2,1)S(1)} %get-tuple-element.7), channel_id=1, source_target_pairs={{8,0},{12,4},{16,8},{20,12},{24,16},{28,20},{32,24},{36,28},{40,32... | collective-permute-start | bytes 786440 | tf_op jit(solution)/shard_map/ppermute | solution.py:37
  121.6 13.9 %collective-permute-start.11 = (bf16[2,128,512]{2,1,0:T(8,128)(2,1)S(1)}, bf16[2,128,512]{2,1,0:T(8,128)(2,1)}, u32[]{:S(2)}, u32[]{:S(2)}) collective-permute-start(bf16[2,128,512]{2,1,0:T(8,128)(2,1)S(1)} %get-tuple-element.8), channel_id=1, source_target_pairs={{0,8},{4,12},{8,16},{12,20},{16,24},{20,28},{24,32},{28,36},{32,40... | collective-permute-start | bytes 786440 | tf_op jit(solution)/shard_map/ppermute | solution.py:37
  125.0 10.6 %collective-permute-start.10 = (bf16[2,128,512]{2,1,0:T(8,128)(2,1)S(1)}, bf16[2,128,512]{2,1,0:T(8,128)(2,1)}, u32[]{:S(2)}, u32[]{:S(2)}) collective-permute-start(bf16[2,128,512]{2,1,0:T(8,128)(2,1)S(1)} %get-tuple-element.9), channel_id=1, source_target_pairs={{4,0},{8,4},{12,8},{16,12},{20,16},{24,20},{28,24},{32,28},{36,32}... | collective-permute-start | bytes 786440 | tf_op jit(solution)/shard_map/ppermute | solution.py:37
  127.8 9.9 %collective-permute-start.9 = (bf16[2,128,512]{2,1,0:T(8,128)(2,1)S(1)}, bf16[2,128,512]{2,1,0:T(8,128)(2,1)}, u32[]{:S(2)}, u32[]{:S(2)}) collective-permute-start(bf16[2,128,512]{2,1,0:T(8,128)(2,1)S(1)} %get-tuple-element.10), channel_id=1, source_target_pairs={{0,4},{4,8},{8,12},{12,16},{16,20},{20,24},{24,28},{28,32},{32,36}... | collective-permute-start | bytes 786440 | tf_op jit(solution)/shard_map/ppermute | solution.py:37
  131.4 7.9 %copy-start.3 = (bf16[1024,3,256]{0,2,1:T(8,128)(2,1)S(1)}, bf16[1024,3,256]{0,2,1:T(8,128)(2,1)}, u32[]{:S(2)}) copy-start(bf16[1024,3,256]{0,2,1:T(8,128)(2,1)} %copy-done.2) | copy-start | bytes 4718596
  139.3 1.4 copy-start.8
Sparse Core Ops, SparseCore 0:
  140.8 36.9 reduce-scatter.1
